TPU v7x, 512 devices: a whole 4x8x8 slice. The times are simulated.
512 devices in a mesh: views: 4 (over x), depth: 32 (over y, z_hi), lat: 4 (over z_lo, core).
Axes of the slice: x: 4, y: 8, z: 8 (z_hi: 4, z_lo: 2; z = z_hi * 2 + z_lo), core: 2. Of those that a mesh axis runs over, the one named last changes fastest.
Arguments:
- density: bfloat16 [64, 2, 128, 2048], P(None, None, 'depth', 'lat'), may hold values from 0 to 3, as said below
- measured: float32 [16, 64, 2048], P('views', None, 'lat'), may hold values from 0 to 4
- shear_shift: int32 [16, 128], P('views', 'depth'), may hold values from -64 to 63
- shear_frac: float32 [16, 128], P('views', 'depth'), may hold values from 0 to 1
- spectrum: float32 [64], replicated, may hold values from 0.05 to 1
- attenuation: float32 [2, 64], replicated, may hold values from 0.3 to 6
Outputs:
- density_gradient: float32 [64, 2, 128, 2048], P('views', None, 'depth', 'lat')
Inputs may be any that keep to these rules, and one draw needn't show every extreme that they name: `density`: densities are non-negative.
All inputs are finite; a program needn't handle non-finite values.
Results may differ from a plain program's by a relative error of at most 0.0016.
Values may be sent and summed in bfloat16 or wider, within the bound.
A program may use at most 64 MiB of HBM per device.

v0:
```python
import jax
import jax.numpy as jnp
from jax import lax
from jax.sharding import PartitionSpec as P

HALO = 64


def with_halo(x, sides, width):
    for axis, dim in sides:
        size, length = (lax.axis_size(axis), x.shape[dim])
        up = [(i, (i + 1) % size) for i in range(size - 1)]
        down = [(j, i) for i, j in up]
        last = lax.slice_in_dim(x, length - width, length, axis=dim)
        first = lax.slice_in_dim(x, 0, width, axis=dim)
        before = lax.ppermute(last, axis, up)
        after = lax.ppermute(first, axis, down)
        x = jnp.concatenate([before, x, after], axis=dim)
    return x


def band_forward(shear_shift, lower_weight, upper_weight, window, block_width):
    band_shape = (shear_shift.shape[1], window, shear_shift.shape[0], block_width)
    tap_index = lax.broadcasted_iota(jnp.int32, band_shape, 1)
    column = lax.broadcasted_iota(jnp.int32, band_shape, 3)
    anchor = (shear_shift.T + HALO)[:, None, :, None]
    nothing = jnp.zeros((), jnp.bfloat16)
    lower_part = jnp.where(tap_index == column + anchor, lower_weight.T[:, None, :, None], nothing)
    upper_part = jnp.where(
        tap_index == column + anchor + 1, upper_weight.T[:, None, :, None], nothing
    )
    return lower_part + upper_part


def band_backward(shear_shift, lower_weight, upper_weight, window, block_width):
    band_shape = (shear_shift.shape[0], window, shear_shift.shape[1], block_width)
    tap_index = lax.broadcasted_iota(jnp.int32, band_shape, 1)
    column = lax.broadcasted_iota(jnp.int32, band_shape, 3)
    anchor = (HALO - shear_shift)[:, None, :, None]
    nothing = jnp.zeros((), jnp.bfloat16)
    lower_part = jnp.where(tap_index == column + anchor, lower_weight[:, None, :, None], nothing)
    upper_part = jnp.where(
        tap_index == column + anchor - 1, upper_weight[:, None, :, None], nothing
    )
    return lower_part + upper_part


def spectral(path_sums, observed, spectrum, attenuation, views_all):
    view_count, row_count, materials, tile_width = path_sums.shape
    block_pixels = 4096
    path_water = path_sums[:, :, 0, :].reshape(-1, block_pixels)
    path_bone = path_sums[:, :, 1, :].reshape(-1, block_pixels)
    target_flat = observed.reshape(-1, block_pixels)
    coefficients = jnp.concatenate(
        [jnp.ones((1, spectrum.shape[0]), jnp.float32), attenuation], axis=0
    )
    emitted = jnp.log(jnp.sum(spectrum))

    def one_block(inputs):
        water_block, bone_block, target_block = inputs
        exponent = (
            attenuation[0][:, None] * water_block[None, :]
            + attenuation[1][:, None] * bone_block[None, :]
        )
        counts = spectrum[:, None] * jnp.exp(-exponent)
        moments = jnp.dot(coefficients, counts, precision=lax.Precision.HIGHEST)
        intensity = moments[0]
        residual = emitted - jnp.log(intensity) - target_block
        factor = residual / intensity / views_all
        return (moments[1:] * factor[None, :]).astype(jnp.bfloat16)

    stacked = lax.map(one_block, (path_water, path_bone, target_flat))
    gradients = jnp.swapaxes(stacked, 0, 1).reshape(materials, view_count, row_count, tile_width)
    return jnp.transpose(gradients, (1, 2, 0, 3))


def per_device(density, measured, shear_shift, shear_frac, spectrum, attenuation):
    row_total, materials, depth_here, tile_width = density.shape
    block_width = min(128, tile_width)
    block_count = tile_width // block_width
    window = block_width + 2 * HALO
    views_all = measured.shape[0] * lax.axis_size("views")
    depth_all = depth_here * lax.axis_size("depth")
    rows_out = row_total // lax.axis_size("views")
    lower_weight = (1.0 - shear_frac).astype(jnp.bfloat16)
    upper_weight = shear_frac.astype(jnp.bfloat16)
    rows_here = density.shape[0]
    padded = with_halo(density, (("lat", 3),), HALO)
    framed = jnp.stack(
        [
            padded[:, :, :, number * block_width : number * block_width + window]
            for number in range(block_count)
        ],
        axis=2,
    )
    forward_band = band_forward(shear_shift, lower_weight, upper_weight, window, block_width)
    partial_value = jnp.einsum(
        "ymnzi,zivc->vymnc", framed, forward_band, preferred_element_type=jnp.float32
    )
    partial_value = partial_value.reshape(shear_shift.shape[0], rows_here, materials, tile_width)
    path_sums = lax.psum(partial_value, "depth") / depth_all
    path_grads = spectral(path_sums, measured, spectrum, attenuation, views_all)
    padded_grads = with_halo(path_grads, (("lat", 3),), HALO)
    framed_grads = jnp.stack(
        [
            padded_grads[:, :, :, number * block_width : number * block_width + window]
            for number in range(block_count)
        ],
        axis=3,
    )
    backward_band = band_backward(shear_shift, lower_weight, upper_weight, window, block_width)
    product = jnp.einsum(
        "vymni,vizc->ymznc", framed_grads, backward_band, preferred_element_type=jnp.float32
    )
    return lax.psum_scatter(
        product.reshape(rows_out * lax.axis_size("views"), materials, depth_here, tile_width),
        "views",
        scatter_dimension=0,
        tiled=True,
    )


def solution(mesh):
    in_specs = (
        P(None, None, "depth", "lat"),
        P("views", None, "lat"),
        P("views", "depth"),
        P("views", "depth"),
        P(),
        P(),
    )
    out_specs = P("views", None, "depth", "lat")
    return jax.shard_map(
        per_device, mesh=mesh, in_specs=in_specs, out_specs=out_specs, check_vma=False
    )
```

profile of v0, /device:TPU:1, one launch (start us, length us, event | category | flops | bytes accessed | tf_op | source)
XLA Modules:
  0.0 428.5 jit_solution(15175280310267215764)
XLA Ops:
  6.5 1.2 copy.23
  7.9 5.4 %collective-permute-start = (bf16[64,2,4,64]{3,0,2,1:T(8,128)(2,1)S(1)}, bf16[64,2,4,64]{3,0,2,1:T(8,128)(2,1)S(1)}, u32[]{:S(2)}, u32[]{:S(2)}) collective-permute-start(bf16[64,2,4,64]{3,0,2,1:T(8,128)(2,1)S(1)} %get-tuple-element.87), channel_id=1, source_target_pairs={{0,1},{1,2},{2,3},{4,5},{5,6},{6,7},{8,9},{9,10},{10,11},{12,13},{... | collective-permute-start | bytes 196616 | tf_op jit(solution)/shard_map/ppermute | solution.py:16
  13.3 4.7 %collective-permute-start.1 = (bf16[64,2,4,64]{3,0,2,1:T(8,128)(2,1)S(1)}, bf16[64,2,4,64]{3,0,2,1:T(8,128)(2,1)S(1)}, u32[]{:S(2)}, u32[]{:S(2)}) collective-permute-start(bf16[64,2,4,64]{3,0,2,1:T(8,128)(2,1)S(1)} %get-tuple-element.88), channel_id=1, source_target_pairs={{1,0},{2,1},{3,2},{5,4},{6,5},{7,6},{9,8},{10,9},{11,10},{13,12},{... | collective-permute-start | bytes 196616 | tf_op jit(solution)/shard_map/ppermute | solution.py:17
  18.0 1.5 collective-permute-done.1
  20.1 1.1 convolution_bitcast_fusion.2
  21.3 1.1 copy.42
  22.5 1.0 copy-done
  24.9 300.5 %all-reduce.3.cloned.1.call-done = f32[4,64,2,512]{3,1,2,0:T(8,128)} async-done(((f32[4,64,2,512]{3,1,2,0:T(8,128)}), f32[4,64,2,512]{3,1,2,0:T(8,128)}) %all-reduce.3.cloned.1.call-update) | async-done | bytes 1048592 | tf_op jit(solution)/shard_map/psum | solution.py:101
  325.3 1.4 broadcast_multiply_fusion
  327.0 35.3 %while.10 = (s32[]{:T(128)}, bf16[32,2,4096]{2,1,0:T(2,128)(2,1)S(1)}, f32[64]{0:T(128)S(1)}, f32[2,64]{1,0:T(2,128)S(1)}, f32[32,4096]{1,0:T(8,128)S(1)}, /*ind...) while((s32[]{:T(128)}, ...), condition=%wide.region_3.4_spmd, body=%wide.region_2.3_spmd.sunk | while | flops 10780674 | bytes 264821 | solution.py:72
  327.1 0.9 convolution_bitcast_fusion.4
  328.2 0.9 convolution_bitcast_fusion.4
  329.3 0.9 convolution_bitcast_fusion.4
  330.4 0.9 convolution_bitcast_fusion.4
  331.5 0.9 convolution_bitcast_fusion.4
  332.6 0.9 convolution_bitcast_fusion.4
  333.7 0.9 convolution_bitcast_fusion.4
  363.0 24.4 %collective-permute-start.2 = (bf16[4,64,2,64]{3,1,0,2:T(8,128)(2,1)S(1)}, bf16[4,64,2,64]{3,1,0,2:T(8,128)(2,1)S(1)}, u32[]{:S(2)}, u32[]{:S(2)}) collective-permute-start(bf16[4,64,2,64]{3,1,0,2:T(8,128)(2,1)S(1)} %get-tuple-element.81), channel_id=1, source_target_pairs={{0,1},{1,2},{2,3},{4,5},{5,6},{6,7},{8,9},{9,10},{10,11},{12,13},{... | collective-permute-start | bytes 196616 | tf_op jit(solution)/shard_map/ppermute | solution.py:16
  387.3 1.9 collective-permute-start.3
  389.6 4.0 collective-permute-done.3
  394.2 1.1 convolution_bitcast_fusion.1
  396.0 1.4 reshape.24
  397.4 22.4 %reduce-scatter.2.cloned.1.call-done = f32[16,2,4,512]{3,0,2,1:T(8,128)} async-done(((f32[64,2,4,512]{3,0,2,1:T(8,128)}), f32[16,2,4,512]{3,0,2,1:T(8,128)}) %reduce-scatter.2.cloned.1.call-update) | async-done | bytes 262160 | tf_op jit(solution)/shard_map/reduce_scatter | solution.py:115
  419.8 1.8 copy.35
  (187 shorter events, 31.5 us)
Async XLA Ops:
  6.5 11.4 %copy-start.2 = (s32[4,4]{1,0:T(4,128)S(1)}, s32[4,4]{1,0:T(4,128)}, u32[]{:S(2)}) copy-start(s32[4,4]{1,0:T(4,128)} %param.10) | copy-start | bytes 196
  6.5 11.5 %copy-start.3 = (f32[4,4]{1,0:T(4,128)S(1)}, f32[4,4]{1,0:T(4,128)}, u32[]{:S(2)}) copy-start(f32[4,4]{1,0:T(4,128)} %param.11) | copy-start | bytes 196
  6.5 318.8 %all-reduce.3.cloned.1.call-start = ((), (), s32[]{:S(2)}) async-start(), calls=%async_computation.1 | async-start | bytes 2097152 | tf_op jit(solution)/shard_map/psum | solution.py:101
  7.9 10.1 %collective-permute-start = (bf16[64,2,4,64]{3,0,2,1:T(8,128)(2,1)S(1)}, bf16[64,2,4,64]{3,0,2,1:T(8,128)(2,1)S(1)}, u32[]{:S(2)}, u32[]{:S(2)}) collective-permute-start(bf16[64,2,4,64]{3,0,2,1:T(8,128)(2,1)S(1)} %get-tuple-element.87), channel_id=1, source_target_pairs={{0,1},{1,2},{2,3},{4,5},{5,6},{6,7},{8,9},{9,10},{10,11},{12,13},{... | collective-permute-start | bytes 196616 | tf_op jit(solution)/shard_map/ppermute | solution.py:16
  13.3 6.3 %collective-permute-start.1 = (bf16[64,2,4,64]{3,0,2,1:T(8,128)(2,1)S(1)}, bf16[64,2,4,64]{3,0,2,1:T(8,128)(2,1)S(1)}, u32[]{:S(2)}, u32[]{:S(2)}) collective-permute-start(bf16[64,2,4,64]{3,0,2,1:T(8,128)(2,1)S(1)} %get-tuple-element.88), channel_id=1, source_target_pairs={{1,0},{2,1},{3,2},{5,4},{6,5},{7,6},{9,8},{10,9},{11,10},{13,12},{... | collective-permute-start | bytes 196616 | tf_op jit(solution)/shard_map/ppermute | solution.py:17
  22.4 1.0 copy-start
  22.4 1.1 copy-start.4
  22.4 2.4 copy-start.1
  22.4 397.4 %reduce-scatter.2.cloned.1.call-start = ((), (), s32[]{:S(2)}) async-start(), calls=%async_computation.2 | async-start | bytes 1310720 | tf_op jit(solution)/shard_map/reduce_scatter | solution.py:115
  363.0 26.6 %collective-permute-start.2 = (bf16[4,64,2,64]{3,1,0,2:T(8,128)(2,1)S(1)}, bf16[4,64,2,64]{3,1,0,2:T(8,128)(2,1)S(1)}, u32[]{:S(2)}, u32[]{:S(2)}) collective-permute-start(bf16[4,64,2,64]{3,1,0,2:T(8,128)(2,1)S(1)} %get-tuple-element.81), channel_id=1, source_target_pairs={{0,1},{1,2},{2,3},{4,5},{5,6},{6,7},{8,9},{9,10},{10,11},{12,13},{... | collective-permute-start | bytes 196616 | tf_op jit(solution)/shard_map/ppermute | solution.py:16
  387.3 6.3 %collective-permute-start.3 = (bf16[4,64,2,64]{3,1,0,2:T(8,128)(2,1)S(1)}, bf16[4,64,2,64]{3,1,0,2:T(8,128)(2,1)S(1)}, u32[]{:S(2)}, u32[]{:S(2)}) collective-permute-start(bf16[4,64,2,64]{3,1,0,2:T(8,128)(2,1)S(1)} %get-tuple-element.82), channel_id=1, source_target_pairs={{1,0},{2,1},{3,2},{5,4},{6,5},{7,6},{9,8},{10,9},{11,10},{13,12},{... | collective-permute-start | bytes 196616 | tf_op jit(solution)/shard_map/ppermute | solution.py:17
Sparse Core Ops, SparseCore 0:
  22.5 302.7 all-reduce.2
  397.6 22.1 reduce-scatter.1
where the time goes:
time: 429 us; the launch traced here: 428 us
  waiting for transfers between devices  328 us (76%)
  starting transfers between devices  36.4 us (8%)
  matrix products  31.8 us (7%)
  between operations  14.3 us (3%)
  local copies, waits for them, and re-layouts  9.82 us (2%)
  other arithmetic  6.36 us (1%)
    psum x1, waiting for transfers between devices, per_device(): path_sums = lax.psum(partial_value, 'depth') / depth_all  300 us
    ppermute x2, starting transfers between devices, with_halo(): before = lax.ppermute(last, axis, up)  29.8 us
    dot_general x32, matrix products, one_block(): moments = jnp.dot(coefficients, counts, precision=lax.Precision.HIGHEST)  29.5 us
    reduce_scatter x1, waiting for transfers between devices, per_device(): lax.psum_scatter(product.reshape(rows_out * lax.axis_size('views'), mater...  22.4 us
  transfers between devices with their start and end apart: 6, of which 4 were waited for; matrix products, arithmetic and copies ran while one was open for 0% of the time, Pallas kernels for 0%

commit v1 on v0

v1 whole, which is shorter than its diff:
```python
import functools

import jax
import jax.numpy as jnp
from jax import lax
from jax.experimental import pallas as pl
from jax.experimental.pallas import tpu as pltpu
from jax.sharding import PartitionSpec as P

HALO = 64
LANES = 128
MESH = pl.DeviceIdType.MESH
(SHX_SEND, SHX_RECV, SH_SEND, SH_RECV, OWN_SEND, LEFT_SEND, RIGHT_SEND, ROWS_LOCAL, ROWS_SEND,
 ROWS_RECV, EDGE_SEND, EDGE_RECV, OUT_SEND, OUT_RECV) = range(14)


def take_lanes(x, index):
    return jnp.take_along_axis(x, index, axis=1, mode="promise_in_bounds")


def kernel(
    sizes, dens, meas, shift, frac, spec, att, out, slabs, planes, rows_in, rows_mine, rows_all,
    shear_x, shear_mine, shear_all, shear_pair, shift_wide, weight_wide, acc, low_rows, up_rows,
    grads, product, sems, own_recv, halo_recv,
):
    group_count, depth_count, lat_count = sizes
    views_here, depth_here, materials = shift.shape[0], shift.shape[1], dens.shape[1]
    rows_here = depth_count // 2
    view_count = group_count * views_here
    pair_count = depth_count // 2
    batches = own_recv.shape[0]
    batch = depth_count // batches
    pairs = batch // 2
    bins = spec.shape[0]
    group = lax.axis_index("views")
    depth = lax.axis_index("depth")
    lat = lax.axis_index("lat")
    half = depth % 2
    has_left = lat > 0
    has_right = lat < lat_count - 1
    halo_from = jnp.where(half == 0, lat - 1, lat + 1)
    has_halo = jnp.where(half == 0, lat, lat_count - 1 - lat) > 0
    halo_to = jnp.where(half == 0, lat + 1, lat - 1)
    gives_halo = jnp.where(half == 0, lat_count - 1 - lat, lat) > 0

    def at(group_to, depth_to, lat_to):
        return {"views": group_to, "depth": depth_to, "lat": lat_to}

    def remote(src, dst, send, recv, to):
        return pltpu.make_async_remote_copy(
            src_ref=src, dst_ref=dst, send_sem=send, recv_sem=recv, device_id=to, device_id_type=MESH
        )

    def drain(ref, sem):
        pltpu.make_async_copy(ref, ref, sem).wait()

    def lanes(start, width):
        return pl.ds(pl.multiple_of(start, LANES), width)

    tile_row = pl.multiple_of((depth // 2) // 8 * 8, 8) if rows_here >= 8 else 0
    tile_rows = rows_in.shape[2]
    row_loads = [
        pltpu.make_async_copy(
            meas.at[:, pl.ds(pl.multiple_of(g * rows_here + tile_row, tile_rows), tile_rows), :],
            rows_in.at[g],
            sems.at[ROWS_LOCAL],
        )
        for g in range(group_count)
    ]
    for load in row_loads:
        load.start()

    barrier = pltpu.get_barrier_semaphore()

    def greet(to):
        pl.semaphore_signal(barrier, inc=1, device_id=to, device_id_type=MESH)

    def greet_depth(k, carry):
        greet(at(group, (depth + k) % depth_count, lat))
        return carry

    lax.fori_loop(1, depth_count, greet_depth, 0)
    for g in range(1, group_count):
        greet(at((group + g) % group_count, depth, lat))

    @pl.when(has_halo)
    def _():
        def greet_halo(k, carry):
            greet(at(group, (depth + k) % depth_count, halo_from))
            return carry

        lax.fori_loop(0, depth_count, greet_halo, 0)
        for g in range(1, group_count):
            greet(at((group + g) % group_count, depth, halo_from))

    sub = lax.broadcasted_iota(jnp.int32, (depth_here, LANES), 0)
    lane4 = lax.broadcasted_iota(jnp.int32, (depth_here, LANES), 1)
    place = lane4 % 32 - group * views_here
    shifts = jnp.zeros((depth_here, LANES), jnp.int32)
    fracs = jnp.zeros((depth_here, LANES), jnp.float32)
    for v in range(views_here):
        for z in range(depth_here):
            here = (sub == z) & (place == v)
            shifts = jnp.where(here, shift[v, z] + HALO, shifts)
            fracs = jnp.where(here, frac[v, z], fracs)
    mine = (place >= 0) & (place < views_here) & (lane4 < 96)
    weights = jnp.where(lane4 < 64, 1.0 - fracs, fracs).astype(jnp.bfloat16).astype(jnp.float32)
    shear_x[group] = jnp.where(mine, jnp.where(lane4 < 32, shifts.astype(jnp.float32), weights), 0.0)

    @pl.when(jnp.logical_not(has_halo) & (half == 0))
    def _():
        slabs[:, :, :, 0:LANES] = jnp.zeros((depth_count, materials, depth_here, LANES), jnp.bfloat16)

    @pl.when(jnp.logical_not(has_halo) & (half == 1))
    def _():
        slabs[:, :, :, 3 * LANES : 4 * LANES] = jnp.zeros(
            (depth_count, materials, depth_here, LANES), jnp.bfloat16
        )

    some = (depth_count + 1) // 2
    expected = (
        depth_count - 1 + group_count - 1
        + jnp.where(has_left, depth_count // 2, 0)
        + jnp.where(has_right, depth_count // 2, 0)
        + jnp.where(gives_halo, group_count - 1, 0)
    )
    pl.semaphore_wait(barrier, expected)

    for g in range(1, group_count):
        remote(
            shear_x.at[group], shear_x.at[group], sems.at[SHX_SEND], sems.at[SHX_RECV],
            at((group + g) % group_count, depth, lat),
        ).start()

    mine_batch = depth // batch

    def own_part(depth_to):
        half_to = depth_to % 2
        src = dens.at[group * rows_here + depth_to // 2, :, :, lanes(half_to * LANES, 3 * LANES)]
        dst = slabs.at[depth, :, :, lanes((1 - half_to) * LANES, 3 * LANES)]
        return src, dst

    def send_own(k, carry):
        depth_to = (depth + k) % depth_count
        src, dst = own_part(depth_to)
        remote(
            src, dst, sems.at[OWN_SEND], own_recv.at[mine_batch], at(group, depth_to, lat)
        ).start()
        return carry

    src, dst = own_part(depth)
    pltpu.make_async_copy(src, dst, own_recv.at[mine_batch]).start()
    lax.fori_loop(1, some, send_own, 0)

    drain(shear_x.at[0 : group_count - 1], sems.at[SHX_RECV])
    table = shear_x[0]
    for g in range(1, group_count):
        table = table + shear_x[g]
    shear_mine[...] = table
    shear_all[depth] = table

    def send_shear(k, carry):
        depth_to = (depth + k) % depth_count
        remote(
            shear_mine, shear_all.at[depth], sems.at[SH_SEND], sems.at[SH_RECV], at(group, depth_to, lat)
        ).start()
        return carry

    lax.fori_loop(1, depth_count, send_shear, 0)
    lax.fori_loop(some, depth_count, send_own, 0)

    @pl.when(has_right)
    def _():
        def send_right(k, carry):
            depth_to = 2 * ((depth // 2 + k) % pair_count)
            remote(
                dens.at[group * rows_here + depth_to // 2, :, :, 3 * LANES : 4 * LANES],
                slabs.at[depth, :, :, 0:LANES],
                sems.at[RIGHT_SEND], halo_recv.at[mine_batch], at(group, depth_to, lat + 1),
            ).start()
            return carry

        lax.fori_loop(0, pair_count, send_right, 0)

    @pl.when(has_left)
    def _():
        def send_left(k, carry):
            depth_to = 2 * ((depth // 2 + k) % pair_count) + 1
            remote(
                dens.at[group * rows_here + depth_to // 2, :, :, 0:LANES],
                slabs.at[depth, :, :, 3 * LANES : 4 * LANES],
                sems.at[LEFT_SEND], halo_recv.at[mine_batch], at(group, depth_to, lat - 1),
            ).start()
            return carry

        lax.fori_loop(0, pair_count, send_left, 0)

    drain(rows_in, sems.at[ROWS_LOCAL])
    row = (depth // 2) % tile_rows
    for g in range(group_count):
        for v in range(views_here):
            rows_mine[g, v : v + 1, :] = rows_in[g, v, pl.ds(row, 1), :]
    for k in range(group_count):
        g = (group + k) % group_count
        src = rows_mine.at[g, :, lanes(half * LANES, 3 * LANES)]
        dst = rows_all.at[group, :, lanes((1 - half) * LANES, 3 * LANES)]
        if k == 0:
            pltpu.make_async_copy(src, dst, sems.at[ROWS_RECV]).start()
        else:
            remote(src, dst, sems.at[ROWS_SEND], sems.at[ROWS_RECV], at(g, depth, lat)).start()

    @pl.when(gives_halo)
    def _():
        for k in range(group_count):
            g = (group + k) % group_count
            remote(
                rows_mine.at[g, :, lanes((1 - half) * (3 * LANES), LANES)],
                rows_all.at[group, :, lanes(half * (3 * LANES), LANES)],
                sems.at[EDGE_SEND], sems.at[EDGE_RECV], at(g, depth, halo_to),
            ).start()

    lane = lax.broadcasted_iota(jnp.int32, (8, LANES), 1)
    drain(shear_all.at[0 : depth_count - 1], sems.at[SH_RECV])

    def join_shear(p, carry):
        shear_pair[p] = jnp.concatenate([shear_all[2 * p], shear_all[2 * p + 1]], axis=0)
        return carry

    lax.fori_loop(0, pair_count, join_shear, 0)

    for t in range(batches):
        b = (mine_batch + t) % batches
        drain(slabs.at[pl.ds(b * batch, batch), :, :, 0 : 3 * LANES], own_recv.at[b])

        @pl.when(has_halo)
        def _():
            drain(slabs.at[pl.ds(b * batch, batch), :, :, 0:LANES], halo_recv.at[b])

        for p in range(pairs):
            for m in range(materials):
                first = slabs[b * batch + 2 * p, m].astype(jnp.float32)
                second = slabs[b * batch + 2 * p + 1, m].astype(jnp.float32)
                planes[p, m] = jnp.concatenate([first, second], axis=0)

        def one_view(v, carry):
            zero = jnp.zeros((8, LANES), jnp.float32)
            low = [[zero if t == 0 else acc[v, m, k] for k in range(3)] for m in range(materials)]
            up = [[zero if t == 0 else acc[v, m, 3 + k] for k in range(4)] for m in range(materials)]
            for p in range(pairs):
                pair = b * pairs + p
                shear = shear_pair[pair]
                pick = jnp.full((8, LANES), v, jnp.int32)
                start = take_lanes(shear, pick).astype(jnp.int32)
                lower = take_lanes(shear, pick + 32)
                upper = take_lanes(shear, pick + 64)
                shift_wide[v, pair] = start
                weight_wide[v, pair, 0] = lower
                weight_wide[v, pair, 1] = upper
                moved = lane + start
                index = moved & (LANES - 1)
                inside = moved < LANES
                for m in range(materials):
                    parts = [
                        take_lanes(planes[p, m, :, k * LANES : (k + 1) * LANES], index) for k in range(4)
                    ]
                    for k in range(3):
                        tap = jnp.where(inside, parts[k], parts[k + 1])
                        low[m][k] = low[m][k] + lower * tap
                        up[m][k] = up[m][k] + upper * tap
                    up[m][3] = up[m][3] + upper * parts[3]
            for m in range(materials):
                for k in range(3):
                    acc[v, m, k] = low[m][k]
                for k in range(4):
                    acc[v, m, 3 + k] = up[m][k]
            return carry

        lax.fori_loop(0, view_count, one_view, 0)

    for v in range(view_count):
        for m in range(materials):
            for k in range(3):
                low_rows[m, v : v + 1, k * LANES : (k + 1) * LANES] = jnp.sum(
                    acc[v, m, k], axis=0, keepdims=True
                )
            for k in range(4):
                up_rows[m, v : v + 1, k * LANES : (k + 1) * LANES] = jnp.sum(
                    acc[v, m, 3 + k], axis=0, keepdims=True
                )
    depth_all = depth_here * depth_count
    paths = [
        (low_rows[m] + pltpu.roll(up_rows[m], 4 * LANES - 1, 1)[:, 0 : 3 * LANES]) * (1.0 / depth_all)
        for m in range(materials)
    ]

    drain(rows_all.at[:, :, 0 : 3 * LANES], sems.at[ROWS_RECV])

    @pl.when(has_halo)
    def _():
        drain(rows_all.at[:, :, 0:LANES], sems.at[EDGE_RECV])

    observed = jnp.concatenate([rows_all[g] for g in range(group_count)], axis=0)
    observed = pltpu.roll(observed, 4 * LANES - HALO, 1)[:, 0 : 3 * LANES]
    blank = jnp.zeros((view_count, 3 * LANES), jnp.float32)

    def one_bin(e, carry):
        intensity, water, bone, total = carry
        counts = spec[e] * jnp.exp(-(att[0, e] * paths[0] + att[1, e] * paths[1]))
        return (
            intensity + counts, water + att[0, e] * counts, bone + att[1, e] * counts, total + spec[e]
        )

    intensity, water, bone, total = lax.fori_loop(
        0, bins, one_bin, (blank, blank, blank, jnp.float32(0.0)), unroll=4
    )
    residual = jnp.log(blank + total) - jnp.log(intensity) - observed
    factor = residual / intensity / view_count
    column = lax.broadcasted_iota(jnp.int32, (view_count, 3 * LANES), 1)
    column = column + (lat * 4 + half * 2) * LANES - HALO
    valid = (column >= 0) & (column < lat_count * 4 * LANES)
    for m, moment in enumerate((water, bone)):
        gradient = jnp.where(valid, (moment * factor).astype(jnp.bfloat16).astype(jnp.float32), 0.0)
        for v in range(view_count):
            for k in range(3):
                grads[m, v, k] = jnp.broadcast_to(
                    gradient[v : v + 1, k * LANES : (k + 1) * LANES], (8, LANES)
                )

    part = pl.ds(pl.multiple_of(half * (2 * LANES), LANES), 2 * LANES)

    def one_pair(t, carry):
        pair = (depth // 2 + 1 + t) % pair_count
        zero = jnp.zeros((8, LANES), jnp.float32)

        def add_view(v, sums):
            moved = lane + (LANES - 1) - shift_wide[v, pair]
            index = moved & (LANES - 1)
            inside = moved < LANES
            lower = weight_wide[v, pair, 0]
            upper = weight_wide[v, pair, 1]
            result = []
            for m in range(materials):
                a0, a1, a2, b0, b1 = sums[m]
                parts = [take_lanes(grads[m, v, k], index) for k in range(3)]
                tap0 = jnp.where(inside, parts[0], parts[1])
                tap1 = jnp.where(inside, parts[1], parts[2])
                result.append((
                    a0 + lower * tap0, a1 + lower * tap1, a2 + lower * parts[2],
                    b0 + upper * tap0, b1 + upper * tap1,
                ))
            return tuple(result)

        sums = lax.fori_loop(0, view_count, add_view, ((zero,) * 5,) * materials, unroll=4)
        for m in range(materials):
            a0, a1, a2, b0, b1 = sums[m]
            ahead = pltpu.roll(jnp.concatenate([a0, a1, a2], axis=1), 3 * LANES - 1, 1)[:, 0 : 2 * LANES]
            result = ahead + jnp.concatenate([b0, b1], axis=1)
            product[2 * pair, m] = result[0:depth_here]
            product[2 * pair + 1, m] = result[depth_here : 2 * depth_here]
        for side in range(2):
            depth_to = 2 * pair + side
            src, dst = product.at[depth_to], out.at[depth // 2, :, :, part]

            @pl.when(depth_to != depth)
            def _():
                remote(src, dst, sems.at[OUT_SEND], sems.at[OUT_RECV], at(group, depth_to, lat)).start()

            @pl.when(depth_to == depth)
            def _():
                pltpu.make_async_copy(src, dst, sems.at[OUT_RECV]).start()

        return carry

    lax.fori_loop(0, pair_count, one_pair, 0)

    others = depth_count - 1
    drain(shear_x.at[0 : group_count - 1], sems.at[SHX_SEND])
    drain(shear_all.at[0:others], sems.at[SH_SEND])
    drain(slabs.at[0:others, :, :, 0 : 3 * LANES], sems.at[OWN_SEND])
    drain(rows_all.at[0 : group_count - 1, :, 0 : 3 * LANES], sems.at[ROWS_SEND])

    @pl.when(has_right)
    def _():
        drain(slabs.at[0:pair_count, :, :, 0:LANES], sems.at[RIGHT_SEND])

    @pl.when(has_left)
    def _():
        drain(slabs.at[0:pair_count, :, :, 0:LANES], sems.at[LEFT_SEND])

    @pl.when(gives_halo)
    def _():
        drain(rows_all.at[:, :, 0:LANES], sems.at[EDGE_SEND])

    drain(product.at[0:others], sems.at[OUT_SEND])
    drain(out, sems.at[OUT_RECV])


def per_device(density, measured, shear_shift, shear_frac, spectrum, attenuation):
    sizes = tuple(lax.axis_size(name) for name in ("views", "depth", "lat"))
    group_count, depth_count, lat_count = sizes
    row_total, materials, depth_here, tile_width = density.shape
    views_here = shear_shift.shape[0]
    view_count = views_here * group_count
    rows_out = row_total // group_count
    pair_count = depth_count // 2
    batch = min(8, depth_count)
    batches = depth_count // batch
    tile_rows = min(8, rows_out)
    f32, bf16 = jnp.float32, jnp.bfloat16
    anywhere = pl.BlockSpec(memory_space=pl.ANY)
    scalars = pl.BlockSpec(memory_space=pltpu.SMEM)
    return pl.pallas_call(
        functools.partial(kernel, sizes),
        out_shape=jax.ShapeDtypeStruct((rows_out, materials, depth_here, tile_width), f32),
        in_specs=[anywhere, anywhere, scalars, scalars, scalars, scalars],
        out_specs=anywhere,
        scratch_shapes=[
            pltpu.VMEM((depth_count, materials, depth_here, tile_width), bf16),
            pltpu.VMEM((batch // 2, materials, 8, tile_width), f32),
            pltpu.VMEM((group_count, views_here, tile_rows, tile_width), f32),
            pltpu.VMEM((group_count, views_here, tile_width), f32),
            pltpu.VMEM((group_count, views_here, tile_width), f32),
            pltpu.VMEM((group_count, depth_here, LANES), f32),
            pltpu.VMEM((depth_here, LANES), f32),
            pltpu.VMEM((depth_count, depth_here, LANES), f32),
            pltpu.VMEM((pair_count, 8, LANES), f32),
            pltpu.VMEM((view_count, pair_count, 8, LANES), jnp.int32),
            pltpu.VMEM((view_count, pair_count, 2, 8, LANES), f32),
            pltpu.VMEM((view_count, materials, 7, 8, LANES), f32),
            pltpu.VMEM((materials, view_count, 3 * LANES), f32),
            pltpu.VMEM((materials, view_count, 4 * LANES), f32),
            pltpu.VMEM((materials, view_count, 3, 8, LANES), f32),
            pltpu.VMEM((depth_count, materials, depth_here, 2 * LANES), f32),
            pltpu.SemaphoreType.DMA((14,)),
            pltpu.SemaphoreType.DMA((batches,)),
            pltpu.SemaphoreType.DMA((batches,)),
        ],
        compiler_params=pltpu.CompilerParams(
            collective_id=0, has_side_effects=True, vmem_limit_bytes=32 * 2**20
        ),
        cost_estimate=pl.CostEstimate(
            flops=16 * 2**20, bytes_accessed=2 * 2**20, transcendentals=2**19
        ),
    )(density, measured, shear_shift, shear_frac, spectrum, attenuation)


def solution(mesh):
    in_specs = (
        P(None, None, "depth", "lat"),
        P("views", None, "lat"),
        P("views", "depth"),
        P("views", "depth"),
        P(),
        P(),
    )
    out_specs = P("views", None, "depth", "lat")
    return jax.shard_map(
        per_device, mesh=mesh, in_specs=in_specs, out_specs=out_specs, check_vma=False
    )
```

time: 429 us -> 64 us (0.15)
  waiting for transfers between devices: 328 us -> 0 us
  Pallas kernels: 0 us -> 58.2 us
  starting transfers between devices: 36.4 us -> 0 us
  matrix products: 31.8 us -> 0 us
  between operations: 14.3 us -> 0.02 us
  other arithmetic: 6.36 us -> 0 us
  local copies, waits for them, and re-layouts: 9.82 us -> 5.48 us
    psum x1 -> x0, waiting for transfers between devices: 300 us -> none  [per_device(): path_sums = lax.psum(partial_value, 'depth') / depth_all]
    pallas_call x0 -> x1, Pallas kernels: none -> 58.2 us  [per_device(): pl.pallas_call(functools.partial(kernel, sizes), out_shape=jax.ShapeDtype...]
    ppermute x4 -> x0, starting transfers between devices: 36.4 us -> none  [the longest x2 29.8 us: with_halo(): before = lax.ppermute(last, axis, up)]
    dot_general x34 -> x0, matrix products: 31.8 us -> none  [the longest x32 29.5 us: one_block(): moments = jnp.dot(coefficients, counts, precision=lax.Precision.HIGHEST)]
    reduce_scatter x1 -> x0, waiting for transfers between devices: 22.4 us -> none  [per_device(): lax.psum_scatter(product.reshape(rows_out * lax.axis_size('views'), mater...]
    ppermute x4 -> x0, waiting for transfers between devices: 5.58 us -> none  [the longest x2 5.58 us: with_halo(): after = lax.ppermute(first, axis, down)]
  transfers between devices with their start and end apart: 6 -> 0, of which waited for: 4 -> 0; matrix products, arithmetic and copies ran while one was open for 0% -> 0% of each run, Pallas kernels for 0% -> 0%
where the time goes in v1:
time: 64 us; the launch traced here: 63.7 us
  Pallas kernels  58.2 us (91%)
  local copies, waits for them, and re-layouts  5.48 us (9%)
    pallas_call x1, Pallas kernels, per_device(): pl.pallas_call(functools.partial(kernel, sizes), out_shape=jax.ShapeDtype...  58.2 us
    unnamed x13, local copies, waits for them, and re-layouts  5.48 us

profile of v1, /device:TPU:1, one launch (start us, length us, event | category | flops | bytes accessed | tf_op | source)
XLA Modules:
  0.0 63.7 jit_solution(7777437850760285363)
XLA Ops:
  0.0 0.0 copy-start
  0.0 1.0 %copy-done = bf16[64,2,4,512]{3,2,1,0:T(4,128)(2,1)S(1)} copy-done((bf16[64,2,4,512]{3,2,1,0:T(4,128)(2,1)S(1)}, bf16[64,2,4,512]{3,2,1,0:T(4,128)(2,1)}, u32[]{:S(2)}) %copy-start) | copy-done | bytes 524312
  1.0 0.0 copy-start.1
  1.0 1.0 %copy-done.1 = f32[4,64,512]{2,1,0:T(8,128)S(1)} copy-done((f32[4,64,512]{2,1,0:T(8,128)S(1)}, f32[4,64,512]{2,1,0:T(8,128)}, u32[]{:S(2)}) %copy-start.1) | copy-done | bytes 524312
  2.1 0.0 copy-start.2
  2.1 0.7 %copy-done.2 = s32[4,4]{1,0:T(4,128)S(1)} copy-done((s32[4,4]{1,0:T(4,128)S(1)}, s32[4,4]{1,0:T(4,128)}, u32[]{:S(2)}) %copy-start.2) | copy-done | bytes 88
  2.8 0.0 copy-start.3
  2.8 0.7 %copy-done.3 = f32[4,4]{1,0:T(4,128)S(1)} copy-done((f32[4,4]{1,0:T(4,128)S(1)}, f32[4,4]{1,0:T(4,128)}, u32[]{:S(2)}) %copy-start.3) | copy-done | bytes 88
  3.4 0.0 copy-start.4
  3.5 0.7 %copy-done.4 = f32[2,64]{1,0:T(2,128)S(1)} copy-done((f32[2,64]{1,0:T(2,128)S(1)}, f32[2,64]{1,0:T(2,128)}, u32[]{:S(2)}) %copy-start.4) | copy-done | bytes 536
  4.1 0.0 copy-start.5
  4.1 0.7 %copy-done.5 = f32[64]{0:T(128)S(1)} copy-done((f32[64]{0:T(128)S(1)}, f32[64]{0:T(128)}, u32[]{:S(2)}) %copy-start.5) | copy-done | bytes 280
  4.8 58.2 %shard_map.64 = f32[16,2,4,512]{3,2,1,0:T(4,128)S(1)} custom-call(bf16[64,2,4,512]{3,2,1,0:T(4,128)(2,1)S(1)} %copy-done, f32[4,64,512]{2,1,0:T(8,128)S(1)} %copy-done.1, s32[4,4]{1,0:T(4,128)S(1)} %copy-done.2, f32[4,4]{1,0:T(4,128)S(1)} %copy-done.3, f32[64]{0:T(128)S(1)} %copy-done.5, f32[2,64]{1,0:T(2,128)S(1)} %copy-done.4), custom_call_target="tpu_custom_call" | custom-call | flops 16777216 | bytes 2097152 | tf_op jit(solution)/shard_map/pallas_call | solution.py:412
  63.0 0.7 %copy.8 = f32[16,2,4,512]{3,2,1,0:T(4,128)} copy(f32[16,2,4,512]{3,2,1,0:T(4,128)S(1)} %shard_map.64) | data formatting | bytes 524288
Async XLA Ops:
  0.0 1.0 %copy-start = (bf16[64,2,4,512]{3,2,1,0:T(4,128)(2,1)S(1)}, bf16[64,2,4,512]{3,2,1,0:T(4,128)(2,1)}, u32[]{:S(2)}) copy-start(bf16[64,2,4,512]{3,2,1,0:T(4,128)(2,1)} %dens.1) | copy-start | bytes 1572868
  1.0 1.0 %copy-start.1 = (f32[4,64,512]{2,1,0:T(8,128)S(1)}, f32[4,64,512]{2,1,0:T(8,128)}, u32[]{:S(2)}) copy-start(f32[4,64,512]{2,1,0:T(8,128)} %meas.1) | copy-start | bytes 1572868
  2.1 0.7 %copy-start.2 = (s32[4,4]{1,0:T(4,128)S(1)}, s32[4,4]{1,0:T(4,128)}, u32[]{:S(2)}) copy-start(s32[4,4]{1,0:T(4,128)} %shift.1) | copy-start | bytes 196
  2.8 0.7 %copy-start.3 = (f32[4,4]{1,0:T(4,128)S(1)}, f32[4,4]{1,0:T(4,128)}, u32[]{:S(2)}) copy-start(f32[4,4]{1,0:T(4,128)} %frac.1) | copy-start | bytes 196
  3.4 0.7 %copy-start.4 = (f32[2,64]{1,0:T(2,128)S(1)}, f32[2,64]{1,0:T(2,128)}, u32[]{:S(2)}) copy-start(f32[2,64]{1,0:T(2,128)} %att.1) | copy-start | bytes 1540
  4.1 0.7 %copy-start.5 = (f32[64]{0:T(128)S(1)}, f32[64]{0:T(128)}, u32[]{:S(2)}) copy-start(f32[64]{0:T(128)} %spec.1) | copy-start | bytes 772

commit v2 on v1

--- a/solution.py
+++ b/solution.py
@@ -10,8 +10,9 @@
 HALO = 64
 LANES = 128
 MESH = pl.DeviceIdType.MESH
+KINDS = 3 * LANES
 (SHX_SEND, SHX_RECV, SH_SEND, SH_RECV, OWN_SEND, LEFT_SEND, RIGHT_SEND, ROWS_LOCAL, ROWS_SEND,
- ROWS_RECV, EDGE_SEND, EDGE_RECV, OUT_SEND, OUT_RECV) = range(14)
+ ROWS_RECV, EDGE_SEND, EDGE_RECV, OUT_SEND, OUT_RECV, OWN_RECV, HALO_RECV) = range(16)
 
 
 def take_lanes(x, index):
@@ -19,18 +20,17 @@
 
 
 def kernel(
-    sizes, dens, meas, shift, frac, spec, att, out, slabs, planes, rows_in, rows_mine, rows_all,
-    shear_x, shear_mine, shear_all, shear_pair, shift_wide, weight_wide, acc, low_rows, up_rows,
-    grads, product, sems, own_recv, halo_recv,
+    sizes, dens, meas, shift_in, frac_in, spec_in, att_in, out, shift, frac, spec, att, slabs, planes, rows_in, rows_mine, rows_all,
+    shear_x, shear_mine, shear_all, spread, shift_wide, weight_wide, acc, low_rows, up_rows,
+    grads, product, sems, small_sems,
 ):
     group_count, depth_count, lat_count = sizes
     views_here, depth_here, materials = shift.shape[0], shift.shape[1], dens.shape[1]
     rows_here = depth_count // 2
     view_count = group_count * views_here
     pair_count = depth_count // 2
-    batches = own_recv.shape[0]
-    batch = depth_count // batches
-    pairs = batch // 2
+    z_count = 4
+    y_count = depth_count // z_count
     bins = spec.shape[0]
     group = lax.axis_index("views")
     depth = lax.axis_index("depth")
@@ -51,6 +51,14 @@
             src_ref=src, dst_ref=dst, send_sem=send, recv_sem=recv, device_id=to, device_id_type=MESH
         )
 
+    def far_first(step, count):
+        return count // 2 + jnp.where(step % 2 == 1, -((step + 1) // 2), step // 2)
+
+    def partner(step):
+        y_to = (depth // z_count + far_first(step // z_count, y_count)) % y_count
+        z_to = (depth % z_count + far_first(step % z_count, z_count)) % z_count
+        return y_to * z_count + z_to
+
     def drain(ref, sem):
         pltpu.make_async_copy(ref, ref, sem).wait()
 
@@ -67,7 +75,11 @@
         )
         for g in range(group_count)
     ]
-    for load in row_loads:
+    small_loads = [
+        pltpu.make_async_copy(src, dst, small_sems.at[k])
+        for k, (src, dst) in enumerate(((shift_in, shift), (frac_in, frac), (spec_in, spec), (att_in, att)))
+    ]
+    for load in small_loads + row_loads:
         load.start()
 
     barrier = pltpu.get_barrier_semaphore()
@@ -96,6 +108,8 @@
     sub = lax.broadcasted_iota(jnp.int32, (depth_here, LANES), 0)
     lane4 = lax.broadcasted_iota(jnp.int32, (depth_here, LANES), 1)
     place = lane4 % 32 - group * views_here
+    for load in small_loads[:2]:
+        load.wait()
     shifts = jnp.zeros((depth_here, LANES), jnp.int32)
     fracs = jnp.zeros((depth_here, LANES), jnp.float32)
     for v in range(views_here):
@@ -107,17 +121,7 @@
     weights = jnp.where(lane4 < 64, 1.0 - fracs, fracs).astype(jnp.bfloat16).astype(jnp.float32)
     shear_x[group] = jnp.where(mine, jnp.where(lane4 < 32, shifts.astype(jnp.float32), weights), 0.0)
 
-    @pl.when(jnp.logical_not(has_halo) & (half == 0))
-    def _():
-        slabs[:, :, :, 0:LANES] = jnp.zeros((depth_count, materials, depth_here, LANES), jnp.bfloat16)
-
-    @pl.when(jnp.logical_not(has_halo) & (half == 1))
-    def _():
-        slabs[:, :, :, 3 * LANES : 4 * LANES] = jnp.zeros(
-            (depth_count, materials, depth_here, LANES), jnp.bfloat16
-        )
-
-    some = (depth_count + 1) // 2
+    some = depth_count // 2
     expected = (
         depth_count - 1 + group_count - 1
         + jnp.where(has_left, depth_count // 2, 0)
@@ -132,25 +136,41 @@
             at((group + g) % group_count, depth, lat),
         ).start()
 
-    mine_batch = depth // batch
-
     def own_part(depth_to):
         half_to = depth_to % 2
         src = dens.at[group * rows_here + depth_to // 2, :, :, lanes(half_to * LANES, 3 * LANES)]
         dst = slabs.at[depth, :, :, lanes((1 - half_to) * LANES, 3 * LANES)]
         return src, dst
 
-    def send_own(k, carry):
-        depth_to = (depth + k) % depth_count
+    def send_halo(depth_to):
+        here = dens.at[group * rows_here + depth_to // 2]
+
+        @pl.when((depth_to % 2 == 0) & has_right)
+        def _():
+            remote(
+                here.at[:, :, 3 * LANES : 4 * LANES], slabs.at[depth, :, :, 0:LANES],
+                sems.at[RIGHT_SEND], sems.at[HALO_RECV], at(group, depth_to, lat + 1),
+            ).start()
+
+        @pl.when((depth_to % 2 == 1) & has_left)
+        def _():
+            remote(
+                here.at[:, :, 0:LANES], slabs.at[depth, :, :, 3 * LANES : 4 * LANES],
+                sems.at[LEFT_SEND], sems.at[HALO_RECV], at(group, depth_to, lat - 1),
+            ).start()
+
+    def send_slab(k, carry):
+        depth_to = partner(k)
         src, dst = own_part(depth_to)
         remote(
-            src, dst, sems.at[OWN_SEND], own_recv.at[mine_batch], at(group, depth_to, lat)
+            src, dst, sems.at[OWN_SEND], sems.at[OWN_RECV], at(group, depth_to, lat)
         ).start()
+        send_halo(depth_to)
         return carry
 
     src, dst = own_part(depth)
-    pltpu.make_async_copy(src, dst, own_recv.at[mine_batch]).start()
-    lax.fori_loop(1, some, send_own, 0)
+    pltpu.make_async_copy(src, dst, sems.at[OWN_RECV]).start()
+    lax.fori_loop(0, some, send_slab, 0)
 
     drain(shear_x.at[0 : group_count - 1], sems.at[SHX_RECV])
     table = shear_x[0]
@@ -160,40 +180,25 @@
     shear_all[depth] = table
 
     def send_shear(k, carry):
-        depth_to = (depth + k) % depth_count
+        depth_to = partner(k)
         remote(
             shear_mine, shear_all.at[depth], sems.at[SH_SEND], sems.at[SH_RECV], at(group, depth_to, lat)
         ).start()
         return carry
 
-    lax.fori_loop(1, depth_count, send_shear, 0)
-    lax.fori_loop(some, depth_count, send_own, 0)
-
-    @pl.when(has_right)
-    def _():
-        def send_right(k, carry):
-            depth_to = 2 * ((depth // 2 + k) % pair_count)
-            remote(
-                dens.at[group * rows_here + depth_to // 2, :, :, 3 * LANES : 4 * LANES],
-                slabs.at[depth, :, :, 0:LANES],
-                sems.at[RIGHT_SEND], halo_recv.at[mine_batch], at(group, depth_to, lat + 1),
-            ).start()
-            return carry
-
-        lax.fori_loop(0, pair_count, send_right, 0)
-
-    @pl.when(has_left)
-    def _():
-        def send_left(k, carry):
-            depth_to = 2 * ((depth // 2 + k) % pair_count) + 1
-            remote(
-                dens.at[group * rows_here + depth_to // 2, :, :, 0:LANES],
-                slabs.at[depth, :, :, 3 * LANES : 4 * LANES],
-                sems.at[LEFT_SEND], halo_recv.at[mine_batch], at(group, depth_to, lat - 1),
-            ).start()
-            return carry
-
-        lax.fori_loop(0, pair_count, send_left, 0)
+    lax.fori_loop(0, depth_count - 1, send_shear, 0)
+    lax.fori_loop(some, depth_count - 1, send_slab, 0)
+    send_halo(depth)
+
+    @pl.when(jnp.logical_not(has_halo) & (half == 0))
+    def _():
+        slabs[:, :, :, 0:LANES] = jnp.zeros((depth_count, materials, depth_here, LANES), jnp.bfloat16)
+
+    @pl.when(jnp.logical_not(has_halo) & (half == 1))
+    def _():
+        slabs[:, :, :, 3 * LANES : 4 * LANES] = jnp.zeros(
+            (depth_count, materials, depth_here, LANES), jnp.bfloat16
+        )
 
     drain(rows_in, sems.at[ROWS_LOCAL])
     row = (depth // 2) % tile_rows
@@ -219,63 +224,65 @@
                 sems.at[EDGE_SEND], sems.at[EDGE_RECV], at(g, depth, halo_to),
             ).start()
 
+    source = lax.broadcasted_iota(jnp.int32, (LANES, KINDS), 0)
+    wanted = lax.broadcasted_iota(jnp.int32, (LANES, KINDS), 1) // LANES * 32
+    for v in range(view_count):
+        spread[v] = (source == wanted + v).astype(jnp.float32).astype(jnp.bfloat16)
+
     lane = lax.broadcasted_iota(jnp.int32, (8, LANES), 1)
     drain(shear_all.at[0 : depth_count - 1], sems.at[SH_RECV])
-
-    def join_shear(p, carry):
-        shear_pair[p] = jnp.concatenate([shear_all[2 * p], shear_all[2 * p + 1]], axis=0)
-        return carry
-
-    lax.fori_loop(0, pair_count, join_shear, 0)
-
-    for t in range(batches):
-        b = (mine_batch + t) % batches
-        drain(slabs.at[pl.ds(b * batch, batch), :, :, 0 : 3 * LANES], own_recv.at[b])
-
-        @pl.when(has_halo)
-        def _():
-            drain(slabs.at[pl.ds(b * batch, batch), :, :, 0:LANES], halo_recv.at[b])
-
-        for p in range(pairs):
+    table = jnp.concatenate([shear_all[p] for p in range(depth_count)], axis=0).astype(jnp.bfloat16)
+
+    def widen(v, carry):
+        wide = jnp.dot(table, spread[v], preferred_element_type=jnp.float32)
+        for p in range(pair_count):
+            rows = wide[8 * p : 8 * p + 8]
+            shift_wide[v, p] = rows[:, 0:LANES].astype(jnp.int32)
+            weight_wide[v, p, 0] = rows[:, LANES : 2 * LANES]
+            weight_wide[v, p, 1] = rows[:, 2 * LANES : 3 * LANES]
+        return carry
+
+    lax.fori_loop(0, view_count, widen, 0, unroll=4)
+
+    drain(slabs.at[:, :, :, 0 : 3 * LANES], sems.at[OWN_RECV])
+
+    @pl.when(has_halo)
+    def _():
+        drain(slabs.at[:, :, :, 0:LANES], sems.at[HALO_RECV])
+
+    for p in range(pair_count):
+        for m in range(materials):
+            first = slabs[2 * p, m].astype(jnp.float32)
+            second = slabs[2 * p + 1, m].astype(jnp.float32)
+            planes[p, m] = jnp.concatenate([first, second], axis=0)
+
+    def one_view(v, carry):
+        zero = jnp.zeros((8, LANES), jnp.float32)
+        low = [[zero] * 3 for m in range(materials)]
+        up = [[zero] * 4 for m in range(materials)]
+        for pair in range(pair_count):
+            moved = lane + shift_wide[v, pair]
+            index = moved & (LANES - 1)
+            inside = moved < LANES
+            lower = weight_wide[v, pair, 0]
+            upper = weight_wide[v, pair, 1]
             for m in range(materials):
-                first = slabs[b * batch + 2 * p, m].astype(jnp.float32)
-                second = slabs[b * batch + 2 * p + 1, m].astype(jnp.float32)
-                planes[p, m] = jnp.concatenate([first, second], axis=0)
-
-        def one_view(v, carry):
-            zero = jnp.zeros((8, LANES), jnp.float32)
-            low = [[zero if t == 0 else acc[v, m, k] for k in range(3)] for m in range(materials)]
-            up = [[zero if t == 0 else acc[v, m, 3 + k] for k in range(4)] for m in range(materials)]
-            for p in range(pairs):
-                pair = b * pairs + p
-                shear = shear_pair[pair]
-                pick = jnp.full((8, LANES), v, jnp.int32)
-                start = take_lanes(shear, pick).astype(jnp.int32)
-                lower = take_lanes(shear, pick + 32)
-                upper = take_lanes(shear, pick + 64)
-                shift_wide[v, pair] = start
-                weight_wide[v, pair, 0] = lower
-                weight_wide[v, pair, 1] = upper
-                moved = lane + start
-                index = moved & (LANES - 1)
-                inside = moved < LANES
-                for m in range(materials):
-                    parts = [
-                        take_lanes(planes[p, m, :, k * LANES : (k + 1) * LANES], index) for k in range(4)
-                    ]
-                    for k in range(3):
-                        tap = jnp.where(inside, parts[k], parts[k + 1])
-                        low[m][k] = low[m][k] + lower * tap
-                        up[m][k] = up[m][k] + upper * tap
-                    up[m][3] = up[m][3] + upper * parts[3]
-            for m in range(materials):
+                parts = [
+                    take_lanes(planes[pair, m, :, k * LANES : (k + 1) * LANES], index) for k in range(4)
+                ]
                 for k in range(3):
-                    acc[v, m, k] = low[m][k]
-                for k in range(4):
-                    acc[v, m, 3 + k] = up[m][k]
-            return carry
-
-        lax.fori_loop(0, view_count, one_view, 0)
+                    tap = jnp.where(inside, parts[k], parts[k + 1])
+                    low[m][k] = low[m][k] + lower * tap
+                    up[m][k] = up[m][k] + upper * tap
+                up[m][3] = up[m][3] + upper * parts[3]
+        for m in range(materials):
+            for k in range(3):
+                acc[v, m, k] = low[m][k]
+            for k in range(4):
+                acc[v, m, 3 + k] = up[m][k]
+        return carry
+
+    lax.fori_loop(0, view_count, one_view, 0)
 
     for v in range(view_count):
         for m in range(materials):
@@ -302,6 +309,8 @@
     observed = jnp.concatenate([rows_all[g] for g in range(group_count)], axis=0)
     observed = pltpu.roll(observed, 4 * LANES - HALO, 1)[:, 0 : 3 * LANES]
     blank = jnp.zeros((view_count, 3 * LANES), jnp.float32)
+    for load in small_loads[2:]:
+        load.wait()
 
     def one_bin(e, carry):
         intensity, water, bone, total = carry
@@ -319,38 +328,35 @@
     column = column + (lat * 4 + half * 2) * LANES - HALO
     valid = (column >= 0) & (column < lat_count * 4 * LANES)
     for m, moment in enumerate((water, bone)):
-        gradient = jnp.where(valid, (moment * factor).astype(jnp.bfloat16).astype(jnp.float32), 0.0)
+        grads[m] = jnp.where(valid, (moment * factor).astype(jnp.bfloat16).astype(jnp.float32), 0.0)
+
+    part = pl.ds(pl.multiple_of(half * (2 * LANES), LANES), 2 * LANES)
+
+    def one_pair(t, carry):
+        y_to = (depth // z_count + far_first(t // 2, y_count)) % y_count
+        pair = y_to * 2 + (depth % z_count // 2 + 1 + t) % 2
+        zero = jnp.zeros((8, LANES), jnp.float32)
+        sums = [(zero,) * 5 for m in range(materials)]
         for v in range(view_count):
-            for k in range(3):
-                grads[m, v, k] = jnp.broadcast_to(
-                    gradient[v : v + 1, k * LANES : (k + 1) * LANES], (8, LANES)
-                )
-
-    part = pl.ds(pl.multiple_of(half * (2 * LANES), LANES), 2 * LANES)
-
-    def one_pair(t, carry):
-        pair = (depth // 2 + 1 + t) % pair_count
-        zero = jnp.zeros((8, LANES), jnp.float32)
-
-        def add_view(v, sums):
             moved = lane + (LANES - 1) - shift_wide[v, pair]
             index = moved & (LANES - 1)
             inside = moved < LANES
             lower = weight_wide[v, pair, 0]
             upper = weight_wide[v, pair, 1]
-            result = []
             for m in range(materials):
                 a0, a1, a2, b0, b1 = sums[m]
-                parts = [take_lanes(grads[m, v, k], index) for k in range(3)]
+                parts = [
+                    take_lanes(
+                        jnp.broadcast_to(grads[m, v : v + 1, k * LANES : (k + 1) * LANES], (8, LANES)), index
+                    )
+                    for k in range(3)
+                ]
                 tap0 = jnp.where(inside, parts[0], parts[1])
                 tap1 = jnp.where(inside, parts[1], parts[2])
-                result.append((
+                sums[m] = (
                     a0 + lower * tap0, a1 + lower * tap1, a2 + lower * parts[2],
                     b0 + upper * tap0, b1 + upper * tap1,
-                ))
-            return tuple(result)
-
-        sums = lax.fori_loop(0, view_count, add_view, ((zero,) * 5,) * materials, unroll=4)
+                )
         for m in range(materials):
             a0, a1, a2, b0, b1 = sums[m]
             ahead = pltpu.roll(jnp.concatenate([a0, a1, a2], axis=1), 3 * LANES - 1, 1)[:, 0 : 2 * LANES]
@@ -403,40 +409,40 @@
     view_count = views_here * group_count
     rows_out = row_total // group_count
     pair_count = depth_count // 2
-    batch = min(8, depth_count)
-    batches = depth_count // batch
     tile_rows = min(8, rows_out)
     f32, bf16 = jnp.float32, jnp.bfloat16
-    anywhere = pl.BlockSpec(memory_space=pl.ANY)
-    scalars = pl.BlockSpec(memory_space=pltpu.SMEM)
+    hbm = pl.BlockSpec(memory_space=pltpu.HBM)
     return pl.pallas_call(
         functools.partial(kernel, sizes),
         out_shape=jax.ShapeDtypeStruct((rows_out, materials, depth_here, tile_width), f32),
-        in_specs=[anywhere, anywhere, scalars, scalars, scalars, scalars],
-        out_specs=anywhere,
+        in_specs=[hbm] * 6,
+        out_specs=pl.BlockSpec(memory_space=pl.ANY),
         scratch_shapes=[
+            pltpu.SMEM(shear_shift.shape, jnp.int32),
+            pltpu.SMEM(shear_frac.shape, f32),
+            pltpu.SMEM(spectrum.shape, f32),
+            pltpu.SMEM(attenuation.shape, f32),
             pltpu.VMEM((depth_count, materials, depth_here, tile_width), bf16),
-            pltpu.VMEM((batch // 2, materials, 8, tile_width), f32),
+            pltpu.VMEM((pair_count, materials, 8, tile_width), f32),
             pltpu.VMEM((group_count, views_here, tile_rows, tile_width), f32),
             pltpu.VMEM((group_count, views_here, tile_width), f32),
             pltpu.VMEM((group_count, views_here, tile_width), f32),
             pltpu.VMEM((group_count, depth_here, LANES), f32),
             pltpu.VMEM((depth_here, LANES), f32),
             pltpu.VMEM((depth_count, depth_here, LANES), f32),
-            pltpu.VMEM((pair_count, 8, LANES), f32),
+            pltpu.VMEM((view_count, LANES, KINDS), bf16),
             pltpu.VMEM((view_count, pair_count, 8, LANES), jnp.int32),
             pltpu.VMEM((view_count, pair_count, 2, 8, LANES), f32),
             pltpu.VMEM((view_count, materials, 7, 8, LANES), f32),
             pltpu.VMEM((materials, view_count, 3 * LANES), f32),
             pltpu.VMEM((materials, view_count, 4 * LANES), f32),
-            pltpu.VMEM((materials, view_count, 3, 8, LANES), f32),
+            pltpu.VMEM((materials, view_count, 3 * LANES), f32),
             pltpu.VMEM((depth_count, materials, depth_here, 2 * LANES), f32),
-            pltpu.SemaphoreType.DMA((14,)),
-            pltpu.SemaphoreType.DMA((batches,)),
-            pltpu.SemaphoreType.DMA((batches,)),
+            pltpu.SemaphoreType.DMA((16,)),
+            pltpu.SemaphoreType.DMA((4,)),
         ],
         compiler_params=pltpu.CompilerParams(
-            collective_id=0, has_side_effects=True, vmem_limit_bytes=32 * 2**20
+            collective_id=0, has_side_effects=True, vmem_limit_bytes=60 * 2**20
         ),
         cost_estimate=pl.CostEstimate(
             flops=16 * 2**20, bytes_accessed=2 * 2**20, transcendentals=2**19

time: 64 us -> 48.9 us (0.76)
  Pallas kernels: 58.2 us -> 47 us
  local copies, waits for them, and re-layouts: 5.48 us -> 1.67 us
    pallas_call x1, Pallas kernels: 58.2 us -> 47 us  [per_device(): pl.pallas_call(functools.partial(kernel, sizes), out_shape=jax.ShapeDtype...]
    unnamed x13 -> x1, local copies, waits for them, and re-layouts: 5.48 us -> 1.67 us
where the time goes in v2:
time: 48.9 us; the launch traced here: 48.7 us
  Pallas kernels  47 us (96%)
  local copies, waits for them, and re-layouts  1.67 us (3%)
    pallas_call x1, Pallas kernels, per_device(): pl.pallas_call(functools.partial(kernel, sizes), out_shape=jax.ShapeDtype...  47 us
    unnamed x1, local copies, waits for them, and re-layouts  1.67 us

profile of v2, /device:TPU:1, one launch (start us, length us, event | category | flops | bytes accessed | tf_op | source)
XLA Modules:
  0.0 48.7 jit_solution(9620849596063307841)
XLA Ops:
  0.0 47.0 %shard_map.64 = f32[16,2,4,512]{3,2,1,0:T(4,128)} custom-call(bf16[64,2,4,512]{3,2,1,0:T(4,128)(2,1)} %dens.1, f32[4,64,512]{2,1,0:T(8,128)} %meas.1, s32[4,4]{1,0:T(4,128)} %shift_in.1, f32[4,4]{1,0:T(4,128)} %frac_in.1, f32[64]{0:T(128)} %spec_in.1, f32[2,64]{1,0:T(2,128)} %att_in.1), custom_call_target="tpu_custom_call" | custom-call | flops 16777216 | bytes 2097152 | tf_op jit(solution)/shard_map/pallas_call | solution.py:415
  47.0 1.7 %copy.8 = f32[16,2,4,512]{3,2,1,0:T(4,128)} copy(f32[16,2,4,512]{3,2,1,0:T(4,128)} %shard_map.64) | data formatting | bytes 524288

commit v3 on v2

--- a/solution.py
+++ b/solution.py
@@ -1,4 +1,5 @@
 import functools
+import math
 
 import jax
 import jax.numpy as jnp
@@ -10,19 +11,32 @@
 HALO = 64
 LANES = 128
 MESH = pl.DeviceIdType.MESH
+FLOOR = 2.0**-17
+STEPS = 32767.0 / math.log(1.0 + 256.0 / FLOOR)
 KINDS = 3 * LANES
 (SHX_SEND, SHX_RECV, SH_SEND, SH_RECV, OWN_SEND, LEFT_SEND, RIGHT_SEND, ROWS_LOCAL, ROWS_SEND,
- ROWS_RECV, EDGE_SEND, EDGE_RECV, OUT_SEND, OUT_RECV, OWN_RECV, HALO_RECV) = range(16)
+ ROWS_RECV, EDGE_SEND, EDGE_RECV, OUT_SEND, OUT_RECV) = range(14)
 
 
 def take_lanes(x, index):
     return jnp.take_along_axis(x, index, axis=1, mode="promise_in_bounds")
+
+
+def encode(x):
+    size = jnp.log(1.0 + jnp.abs(x) * (1.0 / FLOOR)) * STEPS
+    return jnp.round(jnp.where(x < 0.0, -size, size)).astype(jnp.int32).astype(jnp.int16)
+
+
+def decode(code):
+    code = code.astype(jnp.float32)
+    size = (jnp.exp(jnp.abs(code) * (1.0 / STEPS)) - 1.0) * FLOOR
+    return jnp.where(code < 0.0, -size, size)
 
 
 def kernel(
     sizes, dens, meas, shift_in, frac_in, spec_in, att_in, out, shift, frac, spec, att, slabs, planes, rows_in, rows_mine, rows_all,
     shear_x, shear_mine, shear_all, spread, shift_wide, weight_wide, acc, low_rows, up_rows,
-    grads, product, sems, small_sems,
+    grads, product, sems, own_recv, halo_recv, small_sems,
 ):
     group_count, depth_count, lat_count = sizes
     views_here, depth_here, materials = shift.shape[0], shift.shape[1], dens.shape[1]
@@ -31,11 +45,16 @@
     pair_count = depth_count // 2
     z_count = 4
     y_count = depth_count // z_count
+    first_part = 1 + 2 * (y_count // 4) if y_count % 2 == 0 else y_count
+    parts_of = [(0, first_part), (first_part, y_count)] if first_part < y_count else [(0, y_count)]
+    batches = len(parts_of)
+    split = first_part * z_count
     bins = spec.shape[0]
     group = lax.axis_index("views")
     depth = lax.axis_index("depth")
     lat = lax.axis_index("lat")
     half = depth % 2
+    y_here, z_here = lax.div(depth, z_count), lax.rem(depth, z_count)
     has_left = lat > 0
     has_right = lat < lat_count - 1
     halo_from = jnp.where(half == 0, lat - 1, lat + 1)
@@ -52,11 +71,15 @@
         )
 
     def far_first(step, count):
+        if isinstance(step, int):
+            return count // 2 + (-((step + 1) // 2) if step % 2 else step // 2)
         return count // 2 + jnp.where(step % 2 == 1, -((step + 1) // 2), step // 2)
 
     def partner(step):
-        y_to = (depth // z_count + far_first(step // z_count, y_count)) % y_count
-        z_to = (depth % z_count + far_first(step % z_count, z_count)) % z_count
+        y_step = far_first(step // z_count, y_count)
+        z_step = far_first(step % z_count, z_count)
+        y_to = lax.rem(y_here + jnp.where(lat % 2 == 1, y_count - y_step, y_step), y_count)
+        z_to = lax.rem(z_here + jnp.where(lat % 2 == 1, z_count - z_step, z_step), z_count)
         return y_to * z_count + z_to
 
     def drain(ref, sem):
@@ -121,7 +144,7 @@
     weights = jnp.where(lane4 < 64, 1.0 - fracs, fracs).astype(jnp.bfloat16).astype(jnp.float32)
     shear_x[group] = jnp.where(mine, jnp.where(lane4 < 32, shifts.astype(jnp.float32), weights), 0.0)
 
-    some = depth_count // 2
+    some = min(depth_count // 2, split)
     expected = (
         depth_count - 1 + group_count - 1
         + jnp.where(has_left, depth_count // 2, 0)
@@ -142,35 +165,35 @@
         dst = slabs.at[depth, :, :, lanes((1 - half_to) * LANES, 3 * LANES)]
         return src, dst
 
-    def send_halo(depth_to):
+    def send_halo(depth_to, batch):
         here = dens.at[group * rows_here + depth_to // 2]
 
         @pl.when((depth_to % 2 == 0) & has_right)
         def _():
             remote(
                 here.at[:, :, 3 * LANES : 4 * LANES], slabs.at[depth, :, :, 0:LANES],
-                sems.at[RIGHT_SEND], sems.at[HALO_RECV], at(group, depth_to, lat + 1),
+                sems.at[RIGHT_SEND], halo_recv.at[batch], at(group, depth_to, lat + 1),
             ).start()
 
         @pl.when((depth_to % 2 == 1) & has_left)
         def _():
             remote(
                 here.at[:, :, 0:LANES], slabs.at[depth, :, :, 3 * LANES : 4 * LANES],
-                sems.at[LEFT_SEND], sems.at[HALO_RECV], at(group, depth_to, lat - 1),
+                sems.at[LEFT_SEND], halo_recv.at[batch], at(group, depth_to, lat - 1),
             ).start()
 
-    def send_slab(k, carry):
+    def send_slab(batch, k, carry):
         depth_to = partner(k)
         src, dst = own_part(depth_to)
         remote(
-            src, dst, sems.at[OWN_SEND], sems.at[OWN_RECV], at(group, depth_to, lat)
+            src, dst, sems.at[OWN_SEND], own_recv.at[batch], at(group, depth_to, lat)
         ).start()
-        send_halo(depth_to)
+        send_halo(depth_to, batch)
         return carry
 
     src, dst = own_part(depth)
-    pltpu.make_async_copy(src, dst, sems.at[OWN_RECV]).start()
-    lax.fori_loop(0, some, send_slab, 0)
+    pltpu.make_async_copy(src, dst, own_recv.at[batches - 1]).start()
+    lax.fori_loop(0, some, functools.partial(send_slab, 0), 0)
 
     drain(shear_x.at[0 : group_count - 1], sems.at[SHX_RECV])
     table = shear_x[0]
@@ -187,8 +210,9 @@
         return carry
 
     lax.fori_loop(0, depth_count - 1, send_shear, 0)
-    lax.fori_loop(some, depth_count - 1, send_slab, 0)
-    send_halo(depth)
+    lax.fori_loop(some, min(split, depth_count - 1), functools.partial(send_slab, 0), 0)
+    lax.fori_loop(split, depth_count - 1, functools.partial(send_slab, batches - 1), 0)
+    send_halo(depth, batches - 1)
 
     @pl.when(jnp.logical_not(has_halo) & (half == 0))
     def _():
@@ -244,45 +268,52 @@
 
     lax.fori_loop(0, view_count, widen, 0, unroll=4)
 
-    drain(slabs.at[:, :, :, 0 : 3 * LANES], sems.at[OWN_RECV])
-
-    @pl.when(has_halo)
-    def _():
-        drain(slabs.at[:, :, :, 0:LANES], sems.at[HALO_RECV])
-
-    for p in range(pair_count):
-        for m in range(materials):
-            first = slabs[2 * p, m].astype(jnp.float32)
-            second = slabs[2 * p + 1, m].astype(jnp.float32)
-            planes[p, m] = jnp.concatenate([first, second], axis=0)
-
-    def one_view(v, carry):
-        zero = jnp.zeros((8, LANES), jnp.float32)
-        low = [[zero] * 3 for m in range(materials)]
-        up = [[zero] * 4 for m in range(materials)]
-        for pair in range(pair_count):
-            moved = lane + shift_wide[v, pair]
-            index = moved & (LANES - 1)
-            inside = moved < LANES
-            lower = weight_wide[v, pair, 0]
-            upper = weight_wide[v, pair, 1]
+    for batch, (step_from, step_to) in enumerate(parts_of):
+        share = (step_to - step_from) * z_count
+        drain(slabs.at[0:share, :, :, 0 : 3 * LANES], own_recv.at[batch])
+
+        @pl.when(has_halo)
+        def _():
+            drain(slabs.at[0:share, :, :, 0:LANES], halo_recv.at[batch])
+
+        pairs = []
+        for step in range(step_from, step_to):
+            y_step = far_first(step, y_count)
+            y_from = lax.rem(y_here + jnp.where(lat % 2 == 1, y_step, y_count - y_step), y_count)
+            pairs += [2 * y_from, 2 * y_from + 1]
+        for p, pair in enumerate(pairs):
             for m in range(materials):
-                parts = [
-                    take_lanes(planes[pair, m, :, k * LANES : (k + 1) * LANES], index) for k in range(4)
-                ]
+                first = slabs[2 * pair, m].astype(jnp.float32)
+                second = slabs[2 * pair + 1, m].astype(jnp.float32)
+                planes[p, m] = jnp.concatenate([first, second], axis=0)
+
+        def one_view(v, carry):
+            zero = jnp.zeros((8, LANES), jnp.float32)
+            low = [[zero if batch == 0 else acc[v, m, k] for k in range(3)] for m in range(materials)]
+            up = [[zero if batch == 0 else acc[v, m, 3 + k] for k in range(4)] for m in range(materials)]
+            for p, pair in enumerate(pairs):
+                moved = lane + shift_wide[v, pair]
+                index = moved & (LANES - 1)
+                inside = moved < LANES
+                lower = weight_wide[v, pair, 0]
+                upper = weight_wide[v, pair, 1]
+                for m in range(materials):
+                    parts = [
+                        take_lanes(planes[p, m, :, k * LANES : (k + 1) * LANES], index) for k in range(4)
+                    ]
+                    for k in range(3):
+                        tap = jnp.where(inside, parts[k], parts[k + 1])
+                        low[m][k] = low[m][k] + lower * tap
+                        up[m][k] = up[m][k] + upper * tap
+                    up[m][3] = up[m][3] + upper * parts[3]
+            for m in range(materials):
                 for k in range(3):
-                    tap = jnp.where(inside, parts[k], parts[k + 1])
-                    low[m][k] = low[m][k] + lower * tap
-                    up[m][k] = up[m][k] + upper * tap
-                up[m][3] = up[m][3] + upper * parts[3]
-        for m in range(materials):
-            for k in range(3):
-                acc[v, m, k] = low[m][k]
-            for k in range(4):
-                acc[v, m, 3 + k] = up[m][k]
-        return carry
-
-    lax.fori_loop(0, view_count, one_view, 0)
+                    acc[v, m, k] = low[m][k]
+                for k in range(4):
+                    acc[v, m, 3 + k] = up[m][k]
+            return carry
+
+        lax.fori_loop(0, view_count, one_view, 0, unroll=4)
 
     for v in range(view_count):
         for m in range(materials):
@@ -333,7 +364,8 @@
     part = pl.ds(pl.multiple_of(half * (2 * LANES), LANES), 2 * LANES)
 
     def one_pair(t, carry):
-        y_to = (depth // z_count + far_first(t // 2, y_count)) % y_count
+        y_step = far_first(t // 2, y_count)
+        y_to = lax.rem(y_here + jnp.where(lat % 2 == 1, y_count - y_step, y_step), y_count)
         pair = y_to * 2 + (depth % z_count // 2 + 1 + t) % 2
         zero = jnp.zeros((8, LANES), jnp.float32)
         sums = [(zero,) * 5 for m in range(materials)]
@@ -360,7 +392,7 @@
         for m in range(materials):
             a0, a1, a2, b0, b1 = sums[m]
             ahead = pltpu.roll(jnp.concatenate([a0, a1, a2], axis=1), 3 * LANES - 1, 1)[:, 0 : 2 * LANES]
-            result = ahead + jnp.concatenate([b0, b1], axis=1)
+            result = encode(ahead + jnp.concatenate([b0, b1], axis=1))
             product[2 * pair, m] = result[0:depth_here]
             product[2 * pair + 1, m] = result[depth_here : 2 * depth_here]
         for side in range(2):
@@ -377,7 +409,7 @@
 
         return carry
 
-    lax.fori_loop(0, pair_count, one_pair, 0)
+    lax.fori_loop(0, pair_count, one_pair, 0, unroll=2)
 
     others = depth_count - 1
     drain(shear_x.at[0 : group_count - 1], sems.at[SHX_SEND])
@@ -412,9 +444,9 @@
     tile_rows = min(8, rows_out)
     f32, bf16 = jnp.float32, jnp.bfloat16
     hbm = pl.BlockSpec(memory_space=pltpu.HBM)
-    return pl.pallas_call(
+    codes = pl.pallas_call(
         functools.partial(kernel, sizes),
-        out_shape=jax.ShapeDtypeStruct((rows_out, materials, depth_here, tile_width), f32),
+        out_shape=jax.ShapeDtypeStruct((rows_out, materials, depth_here, tile_width), jnp.int16),
         in_specs=[hbm] * 6,
         out_specs=pl.BlockSpec(memory_space=pl.ANY),
         scratch_shapes=[
@@ -437,8 +469,10 @@
             pltpu.VMEM((materials, view_count, 3 * LANES), f32),
             pltpu.VMEM((materials, view_count, 4 * LANES), f32),
             pltpu.VMEM((materials, view_count, 3 * LANES), f32),
-            pltpu.VMEM((depth_count, materials, depth_here, 2 * LANES), f32),
-            pltpu.SemaphoreType.DMA((16,)),
+            pltpu.VMEM((depth_count, materials, depth_here, 2 * LANES), jnp.int16),
+            pltpu.SemaphoreType.DMA((14,)),
+            pltpu.SemaphoreType.DMA((2,)),
+            pltpu.SemaphoreType.DMA((2,)),
             pltpu.SemaphoreType.DMA((4,)),
         ],
         compiler_params=pltpu.CompilerParams(
@@ -448,6 +482,7 @@
             flops=16 * 2**20, bytes_accessed=2 * 2**20, transcendentals=2**19
         ),
     )(density, measured, shear_shift, shear_frac, spectrum, attenuation)
+    return decode(codes)
 
 
 def solution(mesh):

time: 48.9 us -> 45.1 us (0.922)
  Pallas kernels: 47 us -> 43.1 us
  other arithmetic: 0 us -> 1.83 us
  local copies, waits for them, and re-layouts: 1.67 us -> 0 us
    pallas_call x1, Pallas kernels: 47 us -> 43.1 us  [per_device(): pl.pallas_call(functools.partial(kernel, sizes), out_shape=jax.ShapeDtype...]
    select_n x0 -> x1, other arithmetic: none -> 1.83 us  [decode(): return jnp.where(code < 0.0, -size, size)]
    unnamed x1 -> x0, local copies, waits for them, and re-layouts: 1.67 us -> none
where the time goes in v3:
time: 45.1 us; the launch traced here: 45 us
  Pallas kernels  43.1 us (96%)
  other arithmetic  1.83 us (4%)
    pallas_call x1, Pallas kernels, per_device(): pl.pallas_call(functools.partial(kernel, sizes), out_shape=jax.ShapeDtype...  43.1 us
    select_n x1, other arithmetic, decode(): return jnp.where(code < 0.0, -size, size)  1.83 us

profile of v3, /device:TPU:1, one launch (start us, length us, event | category | flops | bytes accessed | tf_op | source)
XLA Modules:
  0.0 45.0 jit_solution(18323039522061524721)
XLA Ops:
  0.0 43.1 %shard_map.64 = s16[16,2,4,512]{3,2,1,0:T(4,128)(2,1)} custom-call(bf16[64,2,4,512]{3,2,1,0:T(4,128)(2,1)} %dens.1, f32[4,64,512]{2,1,0:T(8,128)} %meas.1, s32[4,4]{1,0:T(4,128)} %shift_in.1, f32[4,4]{1,0:T(4,128)} %frac_in.1, f32[64]{0:T(128)} %spec_in.1, f32[2,64]{1,0:T(2,128)} %att_in.1), custom_call_target="tpu_custom_call" | custom-call | flops 16777216 | bytes 2097152 | tf_op jit(solution)/shard_map/pallas_call | solution.py:447
  43.1 1.8 %negate_select_fusion = f32[16,2,4,512]{3,2,1,0:T(4,128)} fusion(s16[16,2,4,512]{3,2,1,0:T(4,128)(2,1)} %shard_map.64), kind=kLoop, calls=%fused_computation | loop fusion | flops 524288 | bytes 393216 | tf_op jit(solution)/shard_map/jit(_where)/select_n | solution.py:33

commit v4 on v3

--- a/solution.py
+++ b/solution.py
@@ -34,7 +34,7 @@
 
 
 def kernel(
-    sizes, dens, meas, shift_in, frac_in, spec_in, att_in, out, shift, frac, spec, att, slabs, planes, rows_in, rows_mine, rows_all,
+    sizes, dens, meas, shift_in, frac_in, spec_in, att_in, out, shift, frac, spec, att, held, slabs, planes, rows_in, rows_mine, rows_all,
     shear_x, shear_mine, shear_all, spread, shift_wide, weight_wide, acc, low_rows, up_rows,
     grads, product, sems, own_recv, halo_recv, small_sems,
 ):
@@ -102,7 +102,8 @@
         pltpu.make_async_copy(src, dst, small_sems.at[k])
         for k, (src, dst) in enumerate(((shift_in, shift), (frac_in, frac), (spec_in, spec), (att_in, att)))
     ]
-    for load in small_loads + row_loads:
+    held_load = pltpu.make_async_copy(dens.at[pl.ds(group * rows_here, rows_here)], held, small_sems.at[4])
+    for load in small_loads[:2]:
         load.start()
 
     barrier = pltpu.get_barrier_semaphore()
@@ -114,7 +115,7 @@
         greet(at(group, (depth + k) % depth_count, lat))
         return carry
 
-    lax.fori_loop(1, depth_count, greet_depth, 0)
+    lax.fori_loop(1, depth_count, greet_depth, 0, unroll=True)
     for g in range(1, group_count):
         greet(at((group + g) % group_count, depth, lat))
 
@@ -124,9 +125,12 @@
             greet(at(group, (depth + k) % depth_count, halo_from))
             return carry
 
-        lax.fori_loop(0, depth_count, greet_halo, 0)
+        lax.fori_loop(0, depth_count, greet_halo, 0, unroll=True)
         for g in range(1, group_count):
             greet(at((group + g) % group_count, depth, halo_from))
+
+    for load in [held_load] + row_loads + small_loads[2:]:
+        load.start()
 
     sub = lax.broadcasted_iota(jnp.int32, (depth_here, LANES), 0)
     lane4 = lax.broadcasted_iota(jnp.int32, (depth_here, LANES), 1)
@@ -151,6 +155,12 @@
         + jnp.where(has_right, depth_count // 2, 0)
         + jnp.where(gives_halo, group_count - 1, 0)
     )
+    held_load.wait()
+    drain(rows_in, sems.at[ROWS_LOCAL])
+    row = (depth // 2) % tile_rows
+    for g in range(group_count):
+        for v in range(views_here):
+            rows_mine[g, v : v + 1, :] = rows_in[g, v, pl.ds(row, 1), :]
     pl.semaphore_wait(barrier, expected)
 
     for g in range(1, group_count):
@@ -161,12 +171,12 @@
 
     def own_part(depth_to):
         half_to = depth_to % 2
-        src = dens.at[group * rows_here + depth_to // 2, :, :, lanes(half_to * LANES, 3 * LANES)]
+        src = held.at[depth_to // 2, :, :, lanes(half_to * LANES, 3 * LANES)]
         dst = slabs.at[depth, :, :, lanes((1 - half_to) * LANES, 3 * LANES)]
         return src, dst
 
     def send_halo(depth_to, batch):
-        here = dens.at[group * rows_here + depth_to // 2]
+        here = held.at[depth_to // 2]
 
         @pl.when((depth_to % 2 == 0) & has_right)
         def _():
@@ -224,11 +234,6 @@
             (depth_count, materials, depth_here, LANES), jnp.bfloat16
         )
 
-    drain(rows_in, sems.at[ROWS_LOCAL])
-    row = (depth // 2) % tile_rows
-    for g in range(group_count):
-        for v in range(views_here):
-            rows_mine[g, v : v + 1, :] = rows_in[g, v, pl.ds(row, 1), :]
     for k in range(group_count):
         g = (group + k) % group_count
         src = rows_mine.at[g, :, lanes(half * LANES, 3 * LANES)]
@@ -454,6 +459,7 @@
             pltpu.SMEM(shear_frac.shape, f32),
             pltpu.SMEM(spectrum.shape, f32),
             pltpu.SMEM(attenuation.shape, f32),
+            pltpu.VMEM((rows_out, materials, depth_here, tile_width), bf16),
             pltpu.VMEM((depth_count, materials, depth_here, tile_width), bf16),
             pltpu.VMEM((pair_count, materials, 8, tile_width), f32),
             pltpu.VMEM((group_count, views_here, tile_rows, tile_width), f32),
@@ -473,7 +479,7 @@
             pltpu.SemaphoreType.DMA((14,)),
             pltpu.SemaphoreType.DMA((2,)),
             pltpu.SemaphoreType.DMA((2,)),
-            pltpu.SemaphoreType.DMA((4,)),
+            pltpu.SemaphoreType.DMA((5,)),
         ],
         compiler_params=pltpu.CompilerParams(
             collective_id=0, has_side_effects=True, vmem_limit_bytes=60 * 2**20

time: 45.1 us -> 44.7 us (level)
  no operation moved by 1% of the time
where the time goes in v4:
time: 44.7 us; the launch traced here: 44.5 us
  Pallas kernels  42.7 us (96%)
  other arithmetic  1.83 us (4%)
    pallas_call x1, Pallas kernels, per_device(): pl.pallas_call(functools.partial(kernel, sizes), out_shape=jax.ShapeDtype...  42.7 us
    select_n x1, other arithmetic, decode(): return jnp.where(code < 0.0, -size, size)  1.83 us

profile of v4, /device:TPU:1, one launch (start us, length us, event | category | flops | bytes accessed | tf_op | source)
XLA Modules:
  0.0 44.5 jit_solution(1335927016355630990)
XLA Ops:
  0.0 42.7 %shard_map.64 = s16[16,2,4,512]{3,2,1,0:T(4,128)(2,1)} custom-call(bf16[64,2,4,512]{3,2,1,0:T(4,128)(2,1)} %dens.1, f32[4,64,512]{2,1,0:T(8,128)} %meas.1, s32[4,4]{1,0:T(4,128)} %shift_in.1, f32[4,4]{1,0:T(4,128)} %frac_in.1, f32[64]{0:T(128)} %spec_in.1, f32[2,64]{1,0:T(2,128)} %att_in.1), custom_call_target="tpu_custom_call" | custom-call | flops 16777216 | bytes 2097152 | tf_op jit(solution)/shard_map/pallas_call | solution.py:452
  42.7 1.8 %negate_select_fusion = f32[16,2,4,512]{3,2,1,0:T(4,128)} fusion(s16[16,2,4,512]{3,2,1,0:T(4,128)(2,1)} %shard_map.64), kind=kLoop, calls=%fused_computation | loop fusion | flops 524288 | bytes 393216 | tf_op jit(solution)/shard_map/jit(_where)/select_n | solution.py:33

commit v5 on v4

--- a/solution.py
+++ b/solution.py
@@ -318,7 +318,7 @@
                     acc[v, m, 3 + k] = up[m][k]
             return carry
 
-        lax.fori_loop(0, view_count, one_view, 0, unroll=4)
+        lax.fori_loop(0, view_count, one_view, 0, unroll=8)
 
     for v in range(view_count):
         for m in range(materials):
@@ -414,7 +414,7 @@
 
         return carry
 
-    lax.fori_loop(0, pair_count, one_pair, 0, unroll=2)
+    lax.fori_loop(0, pair_count, one_pair, 0, unroll=4)
 
     others = depth_count - 1
     drain(shear_x.at[0 : group_count - 1], sems.at[SHX_SEND])

time: 44.7 us -> 44.4 us (level)
  no operation moved by 1% of the time
where the time goes in v5:
time: 44.4 us; the launch traced here: 44.2 us
  Pallas kernels  42.4 us (95%)
  other arithmetic  1.83 us (4%)
    pallas_call x1, Pallas kernels, per_device(): pl.pallas_call(functools.partial(kernel, sizes), out_shape=jax.ShapeDtype...  42.4 us
    select_n x1, other arithmetic, decode(): return jnp.where(code < 0.0, -size, size)  1.83 us

profile of v5, /device:TPU:1, one launch (start us, length us, event | category | flops | bytes accessed | tf_op | source)
XLA Modules:
  0.0 44.2 jit_solution(16921808845426708934)
XLA Ops:
  0.0 42.4 %shard_map.64 = s16[16,2,4,512]{3,2,1,0:T(4,128)(2,1)} custom-call(bf16[64,2,4,512]{3,2,1,0:T(4,128)(2,1)} %dens.1, f32[4,64,512]{2,1,0:T(8,128)} %meas.1, s32[4,4]{1,0:T(4,128)} %shift_in.1, f32[4,4]{1,0:T(4,128)} %frac_in.1, f32[64]{0:T(128)} %spec_in.1, f32[2,64]{1,0:T(2,128)} %att_in.1), custom_call_target="tpu_custom_call" | custom-call | flops 16777216 | bytes 2097152 | tf_op jit(solution)/shard_map/pallas_call | solution.py:452
  42.4 1.8 %negate_select_fusion = f32[16,2,4,512]{3,2,1,0:T(4,128)} fusion(s16[16,2,4,512]{3,2,1,0:T(4,128)(2,1)} %shard_map.64), kind=kLoop, calls=%fused_computation | loop fusion | flops 524288 | bytes 393216 | tf_op jit(solution)/shard_map/jit(_where)/select_n | solution.py:33
